TPU v7x, 512 devices: a whole 4x4x16 slice. The times are simulated.
512 devices in a mesh: pipe: 2 (over z_hi), ctx: 64 (over y, z_lo, core), tp: 4 (over x).
Axes of the slice: x: 4, y: 4, z: 16 (z_hi: 2, z_lo: 8; z = z_hi * 8 + z_lo), core: 2. Of those that a mesh axis runs over, the one named last changes fastest.
Arguments:
- section_output: bfloat16 [2, 8192, 8192], P('pipe', 'ctx', 'tp'), may hold values from -26 to 26
- norm_gain: float32 [2, 8192], P('pipe'), may hold values from 0.1 to 1.9
- kv_weight: bfloat16 [2, 8192, 1024], P('pipe', 'ctx', 'tp'), may hold values from -0.0625 to 0.0625
- queries: bfloat16 [2, 8192, 4096], P('pipe', 'ctx', 'tp'), may hold values from -171 to 171
- rank_block: int32 [128], replicated, may hold values from 0 to 127, each once
Outputs:
- attention: bfloat16 [2, 8192, 4096], P('pipe', 'ctx', 'tp')
- log_total: float32 [2, 8192, 32], P('pipe', 'ctx', 'tp')
Inputs may be any that keep to these rules, and one draw needn't show every extreme that they name: `rank_block`: each of 0 to 127 once.
All inputs are finite; a program needn't handle non-finite values.
Results may differ from a plain program's by a relative error of at most 0.017.
The roundings to bfloat16 on the way count: a program that leaves them out, or rounds other values in their place, can miss the bound.
Values may be sent and summed in bfloat16 or wider, within the bound.
No kernel may reach another device: no remote copies, remote signals or barrier semaphores. Data moves between devices by JAX's collectives and lax.ppermute only.
A program may use at most 128 MiB of HBM per device.

v0:
```python
import math
import jax
import jax.numpy as jnp
from jax import lax
from jax.sharding import PartitionSpec as P

HD = 128
norm_eps = 1e-05
rope_base = 500000.0
mask_fill = -1e30


def passed_along(shard, axis, by):
    peers = lax.axis_size(axis)
    return lax.ppermute(shard, axis, [(i, (i + by) % peers) for i in range(peers)])


def block_positions(rank_block, ctx_count, half_rows):
    block_ids = rank_block.reshape(ctx_count, 2)
    within = jnp.arange(half_rows, dtype=jnp.int32)
    return (block_ids[:, :, None] * half_rows + within[None, None, :]).reshape(-1)


def rotate_keys(raw_keys, positions):
    width = raw_keys.shape[-1]
    half_width = width // 2
    steps_f = jnp.arange(half_width, dtype=jnp.float32)
    inv_freq = jnp.exp(steps_f * (-2.0 / width) * math.log(rope_base))
    angles = positions.astype(jnp.float32)[:, None] * inv_freq[None, :]
    cosine = jnp.cos(angles)
    sine_part = jnp.sin(angles)
    first_half = raw_keys[:, :half_width]
    second_half = raw_keys[:, half_width:]
    return jnp.concatenate(
        [
            first_half * cosine - second_half * sine_part,
            second_half * cosine + first_half * sine_part,
        ],
        axis=1,
    )


def body(section_output, norm_gain, kv_weight, queries, rank_block):
    ctx_count = lax.axis_size("ctx")
    tok_rows = section_output.shape[1]
    half_rows = tok_rows // 2
    head_dim = HD
    head_count = queries.shape[2] // head_dim
    score_scale = 1.0 / math.sqrt(head_dim)
    received = passed_along(section_output, "pipe", 1)
    gathered = lax.all_gather(received, "tp", axis=2, tiled=True)[0].astype(jnp.float32)
    mean_sq = jnp.mean(gathered * gathered, axis=-1, keepdims=True)
    normed = (gathered * lax.rsqrt(mean_sq + norm_eps) * norm_gain[0]).astype(jnp.bfloat16)
    projected = jnp.dot(
        normed,
        lax.all_gather(kv_weight, "ctx", axis=1, tiled=True)[0],
        preferred_element_type=jnp.float32,
    )
    all_pos = block_positions(rank_block, ctx_count, half_rows)
    own_pos = lax.dynamic_slice_in_dim(all_pos, lax.axis_index("ctx") * tok_rows, tok_rows)
    keys = rotate_keys(projected[:, :head_dim], own_pos).astype(jnp.bfloat16)
    values = projected[:, head_dim:].astype(jnp.bfloat16)
    key_values = jnp.concatenate([keys, values], axis=1)
    query_rows = queries[0].reshape(tok_rows, head_count, head_dim)
    halves = (
        (query_rows[:half_rows], own_pos[:half_rows]),
        (query_rows[half_rows:], own_pos[half_rows:]),
    )

    def tile_logits(query_part, query_pos, segment, key_pos):
        logits = (
            jnp.einsum(
                "qhd,kd->hqk", query_part, segment[:, :head_dim], preferred_element_type=jnp.float32
            )
            * score_scale
        )
        allowed = key_pos[None, None, :] <= query_pos[None, :, None]
        return (logits, allowed)

    def weighted_sum(att_weights, segment):
        return jnp.einsum(
            "hqk,kd->qhd",
            att_weights,
            segment[:, head_dim:].astype(jnp.float32),
            precision=lax.Precision.HIGHEST,
        )

    start_pair = (
        jnp.full((head_count, half_rows), mask_fill, jnp.float32),
        jnp.zeros((head_count, half_rows), jnp.float32),
    )
    init_totals = (start_pair, start_pair)
    start_accum = jnp.zeros((half_rows, head_count, head_dim), jnp.float32)
    init_outputs = (start_accum, start_accum)
    segment = lax.all_gather(key_values, "ctx", axis=0, tiled=True)
    key_pos = all_pos
    results = []
    for half_idx in range(2):
        query_part, query_pos = halves[half_idx]

        def update(state_in, query_part=query_part, query_pos=query_pos):
            logits, allowed = tile_logits(query_part, query_pos, segment, key_pos)
            logits = jnp.where(allowed, logits, mask_fill)
            row_max = jnp.maximum(state_in[0], jnp.max(logits, axis=-1))
            row_sum = jnp.sum(jnp.exp(logits - row_max[..., None]), axis=-1)
            return (row_max, row_sum)

        results.append(update(init_totals[half_idx]))
    totals = tuple(results)
    log_halves = tuple((running_pair[0] + jnp.log(running_pair[1]) for running_pair in totals))
    output_segment = lax.all_gather(key_values, "ctx", axis=0, tiled=True)
    results = []
    for half_idx in range(2):
        query_part, query_pos = halves[half_idx]
        log_half = log_halves[half_idx]

        def update(accum, query_part=query_part, query_pos=query_pos, log_half=log_half):
            logits, allowed = tile_logits(query_part, query_pos, output_segment, all_pos)
            att_weights = jnp.where(allowed, jnp.exp(logits - log_half[..., None]), 0.0)
            return weighted_sum(att_weights, output_segment)

        results.append(update(init_outputs[half_idx]))
    outputs = tuple(results)
    attention = (
        jnp.concatenate(outputs, axis=0)
        .astype(jnp.bfloat16)
        .reshape(tok_rows, head_count * head_dim)
    )
    log_total = jnp.concatenate(
        [jnp.transpose(log_halves[0]), jnp.transpose(log_halves[1])], axis=0
    )
    return (attention[None], log_total[None])


def solution(mesh):
    return jax.shard_map(
        body,
        mesh=mesh,
        in_specs=(
            P("pipe", "ctx", "tp"),
            P("pipe", None),
            P("pipe", "ctx", "tp"),
            P("pipe", "ctx", "tp"),
            P(),
        ),
        out_specs=(P("pipe", "ctx", "tp"), P("pipe", "ctx", "tp")),
        check_vma=False,
    )
```

profile of v0, /device:TPU:1, one launch (start us, length us, event | category | flops | bytes accessed | tf_op | source)
XLA Modules:
  0.0 424.6 jit_solution(8950425790996297745)
XLA Ops:
  7.2 0.0 all-gather.4.cloned.1.call-start
  7.2 16.3 %collective-permute-start = (bf16[1,128,2048]{2,1,0:T(8,128)(2,1)}, bf16[1,128,2048]{2,1,0:T(8,128)(2,1)S(1)}, u32[]{:S(2)}, u32[]{:S(2)}) collective-permute-start(bf16[1,128,2048]{2,1,0:T(8,128)(2,1)} %param.5), channel_id=1, source_target_pairs={{0,256},{256,0},{1,257},{257,1},{2,258},{258,2},{3,259},{259,3},{4... | collective-permute-start | bytes 1572872 | tf_op jit(solution)/shard_map/ppermute | solution.py:15
  23.5 15.2 %collective-permute-done = bf16[1,128,2048]{2,1,0:T(8,128)(2,1)S(1)} collective-permute-done((bf16[1,128,2048]{2,1,0:T(8,128)(2,1)}, bf16[1,128,2048]{2,1,0:T(8,128)(2,1)S(1)}, u32[]{:S(2)}, u32[]{:S(2)}) %collective-permute-start) | collective-permute-done | bytes 524320 | tf_op jit(solution)/shard_map/ppermute | solution.py:15
  38.7 0.0 copy-start.1
  38.7 0.8 copy-done.1
  39.5 0.0 all-gather.4.cloned.1.call-update
  39.5 0.0 all-gather.6.cloned.1.call-start
  39.6 0.7 all-gather.6.cloned.1.call-update
  40.3 0.0 all-gather.8.cloned.1.call-start
  40.3 0.7 broadcast_multiply_fusion
  41.0 0.1 mul.100
  41.1 0.1 iota_add_fusion
  41.3 0.1 add.65
  41.4 0.1 fusion.57
  41.5 68.4 %all-gather.4.cloned.1.call-done = bf16[1,128,8192]{2,1,0:T(8,128)(2,1)} async-done(((bf16[1,128,2048]{2,1,0:T(8,128)(2,1)}), bf16[1,128,8192]{2,1,0:T(8,128)(2,1)}) %all-gather.4.cloned.1.call-update) | async-done | bytes 2097168 | tf_op jit(solution)/shard_map/all_gather | solution.py:51
  109.8 2.1 fusion.20
  111.9 123.5 %all-gather.6.cloned.1.call-done = bf16[1,8192,256]{2,1,0:T(8,128)(2,1)} async-done(((bf16[1,128,256]{2,1,0:T(8,128)(2,1)}), bf16[1,8192,256]{2,1,0:T(8,128)(2,1)}) %all-gather.6.cloned.1.call-update) | async-done | bytes 4194320 | tf_op jit(solution)/shard_map/all_gather | solution.py:56
  235.4 3.6 fusion.23
  239.0 0.1 fusion.58
  239.1 0.1 copy.20
  239.2 0.1 copy.19
  239.3 0.2 fusion.50
  239.5 0.1 copy.13
  239.6 0.1 copy.14
  239.7 0.7 pad_maximum_fusion.1
  240.5 0.0 all-gather.8.cloned.1.call-update
  240.5 1.0 slice_bitcast_fusion.15
  241.5 0.1 fusion.59
  241.6 0.6 broadcast_compare_fusion.1
  242.3 116.9 %all-gather.8.cloned.1.call-done = bf16[8192,256]{1,0:T(8,128)(2,1)} async-done(((bf16[128,256]{1,0:T(8,128)(2,1)}), bf16[8192,256]{1,0:T(8,128)(2,1)}) %all-gather.8.cloned.1.call-update) | async-done | bytes 4194320 | tf_op jit(solution)/shard_map/all_gather | solution.py:111
  359.2 0.0 copy-start.2
  359.2 9.1 %fusion.8 = (f32[8,64]{1,0:T(8,128)S(1)}, f32[8192,64,8]{0,1,2:T(8,128)}) fusion(pred[64,8192]{1,0:T(8,128)(4,1)S(1)} %get-tuple-element.10, bf16[64,8,128]{2,1,0:T(8,128)(2,1)S(1)} %bitcast.76, bf16[8192,256]{1,0:T(8,128)(2,1)} %all-gather.8.cloned.1.call-done), kind=kOutput, calls=%fused_computation.12 | convolution fusion | flops 1086324224 | bytes 19531776 | tf_op jit(solution)/shard_map/qhd,kd->hqk/dot_general | solution.py:72
  368.3 0.0 copy-done.2
  368.3 3.1 fusion.9
  371.4 0.0 copy-start
  371.4 16.4 %exponential_reduce_fusion = (f32[8,64]{1,0:T(8,128)S(1)}, f32[8,64]{1,0:T(8,128)S(1)}) fusion(f32[8192,64,8]{0,1,2:T(8,128)S(1)} %get-tuple-element.15, f32[8,64]{1,0:T(8,128)S(1)} %broadcast_maximum_fusion, pred[64,8192]{1,0:T(8,128)(4,1)S(1)} %get-tuple-element.11, f32[8,64]{1,0:T(8,128)S(1)} %broadcast_maximum_fusion.1, ...), kind=kLoop, calls=%fused_computation.10 | loop fusion | flops 33553408 | bytes 34611200 | tf_op jit(solution)/shard_map/reduce_sum | solution.py:105
  387.8 0.0 copy-done
  387.8 14.0 %fusion.40 = bf16[64,8,128]{2,0,1:T(8,128)(2,1)S(1)} fusion(f32[8192,64,8]{0,1,2:T(8,128)} %get-tuple-element.17, f32[8,64]{1,0:T(8,128)S(1)} %log_add_fusion.1, pred[64,8192]{1,0:T(8,128)(4,1)S(1)} %get-tuple-element.10, bf16[8192,256]{1,0:T(8,128)(2,1)S(1)} %copy-done.2), kind=kOutput, calls=%fused_computation.41 | convolution fusion | flops 6455099392 | bytes 19533824 | tf_op jit(solution)/shard_map/hqk,kd->qhd/dot_general | solution.py:81
  401.9 0.1 copy.16
  402.0 0.1 concatenate.25
  402.1 14.4 %fusion.37 = bf16[64,8,128]{2,0,1:T(8,128)(2,1)S(1)} fusion(f32[8192,64,8]{0,1,2:T(8,128)} %copy-done, f32[8,64]{1,0:T(8,128)S(1)} %log_add_fusion, pred[64,8192]{1,0:T(8,128)(4,1)S(1)} %get-tuple-element.11, bf16[8192,256]{1,0:T(8,128)(2,1)} %all-gather.8.cloned.1.call-done), kind=kOutput, calls=%fused_computation.40 | convolution fusion | flops 6455099392 | bytes 19531776 | tf_op jit(solution)/shard_map/hqk,kd->qhd/dot_general | solution.py:81
  416.5 0.1 copy.18
  416.6 0.1 concatenate.26
  416.7 0.7 pad_maximum_fusion
  417.4 0.7 maximum_bitcast_fusion
  (9 shorter events, 0.1 us)
Async XLA Ops:
  7.2 102.7 %all-gather.4.cloned.1.call-start = ((), (), s32[]{:S(2)}) async-start(), calls=%async_computation | async-start | bytes 2621440 | tf_op jit(solution)/shard_map/all_gather | solution.py:51
  7.2 31.5 %collective-permute-start = (bf16[1,128,2048]{2,1,0:T(8,128)(2,1)}, bf16[1,128,2048]{2,1,0:T(8,128)(2,1)S(1)}, u32[]{:S(2)}, u32[]{:S(2)}) collective-permute-start(bf16[1,128,2048]{2,1,0:T(8,128)(2,1)} %param.5), channel_id=1, source_target_pairs={{0,256},{256,0},{1,257},{257,1},{2,258},{258,2},{3,259},{259,3},{4... | collective-permute-start | bytes 1572872 | tf_op jit(solution)/shard_map/ppermute | solution.py:15
  38.7 0.8 copy-start.1
  39.5 195.9 %all-gather.6.cloned.1.call-start = ((), (), s32[]{:S(2)}) async-start(), calls=%async_computation.1 | async-start | bytes 4259840 | tf_op jit(solution)/shard_map/all_gather | solution.py:56
  40.3 318.9 %all-gather.8.cloned.1.call-start = ((), (), s32[]{:S(2)}) async-start(), calls=%async_computation.2 | async-start | bytes 4259840 | tf_op jit(solution)/shard_map/all_gather | solution.py:111
  359.2 9.1 %copy-start.2 = (bf16[8192,256]{1,0:T(8,128)(2,1)S(1)}, bf16[8192,256]{1,0:T(8,128)(2,1)}, u32[]{:S(2)}) copy-start(bf16[8192,256]{1,0:T(8,128)(2,1)} %all-gather.8.cloned.1.call-done) | copy-start | bytes 12582916
  371.4 16.4 %copy-start = (f32[8192,64,8]{0,1,2:T(8,128)}, f32[8192,64,8]{0,1,2:T(8,128)S(1)}, u32[]{:S(2)}) copy-start(f32[8192,64,8]{0,1,2:T(8,128)S(1)} %get-tuple-element.15) | copy-start | bytes 50331652
Sparse Core Ops, SparseCore 0:
  39.7 70.1 all-gather.3
  112.0 123.3 all-gather.5
  240.6 118.5 all-gather.7
where the time goes:
time: 425 us
  waiting for transfers between devices  325 us (76%)
  matrix products  44.3 us (10%)
  other arithmetic  22.4 us (5%)
  starting transfers between devices  16.4 us (4%)
  between operations  13.9 us (3%)
    all_gather x1, waiting for transfers between devices, body(): lax.all_gather(kv_weight, 'ctx', axis=1, tiled=True)[0]  123 us
    all_gather x1, waiting for transfers between devices, body(): output_segment = lax.all_gather(key_values, 'ctx', axis=0, tiled=True)  117 us
    all_gather x1, waiting for transfers between devices, body(): lax.all_gather(received, 'tp', axis=2, tiled=True)[0].astype(jnp.float32)  68.4 us
    dot_general x2, matrix products, weighted_sum(): jnp.einsum('hqk,kd->qhd', att_weights, segment[:, head_dim:].astype(jnp.f...  28.5 us
    reduce_sum x1, other arithmetic, update(): row_sum = jnp.sum(jnp.exp(logits - row_max[..., None]), axis=-1)  16.4 us
    ppermute x1, starting transfers between devices, passed_along(): lax.ppermute(shard, axis, [(i, (i + by) % peers) for i in range(peers)])  16.3 us
    ppermute x1, waiting for transfers between devices, passed_along(): lax.ppermute(shard, axis, [(i, (i + by) % peers) for i in range(peers)])  15.2 us
    dot_general x2, matrix products, tile_logits(): jnp.einsum('qhd,kd->hqk', query_part, segment[:, :head_dim], preferred_el...  12.2 us
  transfers between devices with their start and end apart: 4, of which 4 were waited for; matrix products, arithmetic and copies ran while one was open for 1% of the time, Pallas kernels for 0%

commit v1 on v0

--- a/solution.py
+++ b/solution.py
@@ -8,6 +8,24 @@
 norm_eps = 1e-05
 rope_base = 500000.0
 mask_fill = -1e30
+
+
+def ring_gather(array, axis, dim):
+    ways, here, hop = (lax.axis_size(axis), lax.axis_index(axis), array.shape[dim])
+    dims = [n * ways if d == dim else n for d, n in enumerate(array.shape)]
+    full = lax.dynamic_update_slice_in_dim(
+        jnp.zeros(dims, array.dtype), array, here * hop, axis=dim
+    )
+    going_up = going_down = array
+    for far in range(1, ways // 2 + 1):
+        going_up = lax.ppermute(going_up, axis, [(d, (d + 1) % ways) for d in range(ways)])
+        full = lax.dynamic_update_slice_in_dim(full, going_up, (here - far) % ways * hop, axis=dim)
+        if 2 * far < ways:
+            going_down = lax.ppermute(going_down, axis, [(d, (d - 1) % ways) for d in range(ways)])
+            full = lax.dynamic_update_slice_in_dim(
+                full, going_down, (here + far) % ways * hop, axis=dim
+            )
+    return full
 
 
 def passed_along(shard, axis, by):
@@ -48,7 +66,7 @@
     head_count = queries.shape[2] // head_dim
     score_scale = 1.0 / math.sqrt(head_dim)
     received = passed_along(section_output, "pipe", 1)
-    gathered = lax.all_gather(received, "tp", axis=2, tiled=True)[0].astype(jnp.float32)
+    gathered = ring_gather(received, "tp", 2)[0].astype(jnp.float32)
     mean_sq = jnp.mean(gathered * gathered, axis=-1, keepdims=True)
     normed = (gathered * lax.rsqrt(mean_sq + norm_eps) * norm_gain[0]).astype(jnp.bfloat16)
     projected = jnp.dot(

time: 425 us -> 357 us (0.84)
  waiting for transfers between devices: 325 us -> 253 us
  starting transfers between devices: 16.4 us -> 24.7 us
  other arithmetic: 22.4 us -> 16 us
    all_gather x1 -> x0, waiting for transfers between devices: 68.4 us -> none  [body(): lax.all_gather(received, 'tp', axis=2, tiled=True)[0].astype(jnp.float32)]
    all_gather x1, waiting for transfers between devices: 123 us -> 106 us  [body(): lax.all_gather(kv_weight, 'ctx', axis=1, tiled=True)[0]]
    ppermute x0 -> x3, waiting for transfers between devices: none -> 13.4 us  [the longest x2 12.9 us: ring_gather(): lax.ppermute(going_up, axis, [(d, (d + 1) % ways) for d in range(ways)])]
    ppermute x0 -> x3, starting transfers between devices: none -> 8.39 us  [the longest x2 5.02 us: ring_gather(): lax.ppermute(going_up, axis, [(d, (d + 1) % ways) for d in range(ways)])]
    reduce_sum x1, other arithmetic: 16.4 us -> 11.6 us  [update(): row_sum = jnp.sum(jnp.exp(logits - row_max[..., None]), axis=-1)]
  transfers between devices with their start and end apart: 4 -> 6, of which waited for: 4 -> 6; matrix products, arithmetic and copies ran while one was open for 1% -> 1% of each run, Pallas kernels for 0% -> 0%
where the time goes in v1:
time: 357 us
  waiting for transfers between devices  253 us (71%)
  matrix products  44.3 us (12%)
  starting transfers between devices  24.7 us (7%)
  other arithmetic  16 us (4%)
  between operations  14.4 us (4%)
  local copies, waits for them, and re-layouts  4.47 us (1%)
    all_gather x1, waiting for transfers between devices, body(): output_segment = lax.all_gather(key_values, 'ctx', axis=0, tiled=True)  117 us
    all_gather x1, waiting for transfers between devices, body(): lax.all_gather(kv_weight, 'ctx', axis=1, tiled=True)[0]  106 us
    dot_general x2, matrix products, weighted_sum(): jnp.einsum('hqk,kd->qhd', att_weights, segment[:, head_dim:].astype(jnp.f...  28.7 us
    ppermute x1, starting transfers between devices, passed_along(): lax.ppermute(shard, axis, [(i, (i + by) % peers) for i in range(peers)])  16.3 us
    ppermute x1, waiting for transfers between devices, passed_along(): lax.ppermute(shard, axis, [(i, (i + by) % peers) for i in range(peers)])  15.5 us
    ppermute x2, waiting for transfers between devices, ring_gather(): lax.ppermute(going_up, axis, [(d, (d + 1) % ways) for d in range(ways)])  12.9 us
    dot_general x2, matrix products, tile_logits(): jnp.einsum('qhd,kd->hqk', query_part, segment[:, :head_dim], preferred_el...  12.6 us
    reduce_sum x1, other arithmetic, update(): row_sum = jnp.sum(jnp.exp(logits - row_max[..., None]), axis=-1)  11.6 us
  transfers between devices with their start and end apart: 6, of which 6 were waited for; matrix products, arithmetic and copies ran while one was open for 1% of the time, Pallas kernels for 0%

profile of v1, /device:TPU:1, one launch (start us, length us, event | category | flops | bytes accessed | tf_op | source)
XLA Modules:
  0.0 356.8 jit_solution(10648757309520072343)
XLA Ops:
  7.2 0.0 all-gather.3.cloned.1.call-start
  7.2 0.7 all-gather.3.cloned.1.call-update
  7.9 0.0 all-gather.5.cloned.1.call-start
  7.9 16.3 %collective-permute-start = (bf16[1,128,2048]{2,1,0:T(8,128)(2,1)}, bf16[1,128,2048]{2,1,0:T(8,128)(2,1)S(1)}, u32[]{:S(2)}, u32[]{:S(2)}) collective-permute-start(bf16[1,128,2048]{2,1,0:T(8,128)(2,1)} %param.5), channel_id=1, source_target_pairs={{0,256},{256,0},{1,257},{257,1},{2,258},{258,2},{3,259},{259,3},{4... | collective-permute-start | bytes 1572872 | tf_op jit(solution)/shard_map/ppermute | solution.py:33
  24.2 0.7 broadcast_multiply_fusion
  24.9 0.1 mul.113
  25.0 0.1 iota_add_fusion
  25.2 0.1 add.100
  25.3 0.1 fusion.56
  25.3 15.5 %collective-permute-done = bf16[1,128,2048]{2,1,0:T(8,128)(2,1)S(1)} collective-permute-done((bf16[1,128,2048]{2,1,0:T(8,128)(2,1)}, bf16[1,128,2048]{2,1,0:T(8,128)(2,1)S(1)}, u32[]{:S(2)}, u32[]{:S(2)}) %collective-permute-start) | collective-permute-done | bytes 524320 | tf_op jit(solution)/shard_map/ppermute | solution.py:33
  40.8 3.1 collective-permute-start.1
  44.0 0.0 copy-start.3
  44.0 3.4 collective-permute-start.2
  47.4 0.2 squeeze.14
  47.6 0.1 bitcast_dynamic-update-slice_fusion.3
  47.7 4.3 %collective-permute-done.1 = bf16[1,128,2048]{2,1,0:T(8,128)(2,1)S(1)} collective-permute-done((bf16[1,128,2048]{2,1,0:T(8,128)(2,1)S(1)}, bf16[1,128,2048]{2,1,0:T(8,128)(2,1)S(1)}, u32[]{:S(2)}, u32[]{:S(2)}) %collective-permute-start.1) | collective-permute-done | bytes 524320 | tf_op jit(solution)/shard_map/ppermute | solution.py:21
  52.0 1.9 collective-permute-start.3
  53.9 0.1 bitcast_dynamic-update-slice_fusion.2
  53.9 0.4 collective-permute-done.2
  54.4 8.7 %collective-permute-done.3 = bf16[1,128,2048]{2,1,0:T(8,128)(2,1)S(1)} collective-permute-done((bf16[1,128,2048]{2,1,0:T(8,128)(2,1)S(1)}, bf16[1,128,2048]{2,1,0:T(8,128)(2,1)S(1)}, u32[]{:S(2)}, u32[]{:S(2)}) %collective-permute-start.3) | collective-permute-done | bytes 524320 | tf_op jit(solution)/shard_map/ppermute | solution.py:21
  63.1 0.1 bitcast_dynamic-update-slice_fusion
  63.1 0.5 fusion.20
  63.7 106.5 %all-gather.3.cloned.1.call-done = bf16[1,8192,256]{2,1,0:T(8,128)(2,1)} async-done(((bf16[1,128,256]{2,1,0:T(8,128)(2,1)}), bf16[1,8192,256]{2,1,0:T(8,128)(2,1)}) %all-gather.3.cloned.1.call-update) | async-done | bytes 4194320 | tf_op jit(solution)/shard_map/all_gather | solution.py:74
  170.1 0.0 copy-done.3
  170.1 0.0 copy-start.1
  170.1 3.0 fusion.23
  173.2 0.1 fusion.57
  173.3 0.1 copy.20
  173.3 0.1 copy.19
  173.4 0.2 fusion.49
  173.7 0.1 copy.13
  173.8 0.1 copy.14
  173.9 0.7 pad_maximum_fusion.1
  174.6 0.0 all-gather.5.cloned.1.call-update
  174.7 0.0 copy-done.1
  174.8 0.1 fusion.58
  174.8 0.6 broadcast_compare_fusion.1
  175.5 116.9 %all-gather.5.cloned.1.call-done = bf16[8192,256]{1,0:T(8,128)(2,1)} async-done(((bf16[128,256]{1,0:T(8,128)(2,1)}), bf16[8192,256]{1,0:T(8,128)(2,1)}) %all-gather.5.cloned.1.call-update) | async-done | bytes 4194320 | tf_op jit(solution)/shard_map/all_gather | solution.py:129
  292.4 0.0 copy-start.2
  292.4 4.8 %fusion.9 = (f32[8,64]{1,0:T(8,128)S(1)}, f32[8192,64,8]{0,1,2:T(8,128)S(1)}) fusion(pred[64,8192]{1,0:T(8,128)(4,1)S(1)} %get-tuple-element.11, bf16[64,8,128]{2,1,0:T(8,128)(2,1)S(1)} %bitcast.81, bf16[8192,256]{1,0:T(8,128)(2,1)} %all-gather.5.cloned.1.call-done), kind=kOutput, calls=%fused_computation.13 | convolution fusion | flops 1086324224 | bytes 19531776 | tf_op jit(solution)/shard_map/qhd,kd->hqk/dot_general | solution.py:90
  297.2 0.0 copy-start
  297.2 0.0 copy-done.2
  297.2 7.8 %fusion.8 = (f32[8,64]{1,0:T(8,128)S(1)}, f32[8192,64,8]{0,1,2:T(8,128)}) fusion(pred[64,8192]{1,0:T(8,128)(4,1)S(1)} %get-tuple-element.10, bf16[64,8,128]{2,1,0:T(8,128)(2,1)S(1)} %bitcast.80, bf16[8192,256]{1,0:T(8,128)(2,1)S(1)} %copy-done.2), kind=kOutput, calls=%fused_computation.12 | convolution fusion | flops 1086324224 | bytes 19531776 | tf_op jit(solution)/shard_map/qhd,kd->hqk/dot_general | solution.py:90
  305.0 2.9 copy-done
  307.9 11.6 %exponential_reduce_fusion = (f32[8,64]{1,0:T(8,128)S(1)}, f32[8,64]{1,0:T(8,128)S(1)}) fusion(f32[8192,64,8]{0,1,2:T(8,128)S(1)} %get-tuple-element.15, f32[8,64]{1,0:T(8,128)S(1)} %broadcast_maximum_fusion, pred[64,8192]{1,0:T(8,128)(4,1)S(1)} %get-tuple-element.11, f32[8,64]{1,0:T(8,128)S(1)} %broadcast_maximum_fusion.1, ...), kind=kLoop, calls=%fused_computation.10 | loop fusion | flops 33553408 | bytes 34611200 | tf_op jit(solution)/shard_map/reduce_sum | solution.py:123
  319.5 14.0 %fusion.39 = bf16[64,8,128]{2,0,1:T(8,128)(2,1)S(1)} fusion(f32[8192,64,8]{0,1,2:T(8,128)} %get-tuple-element.17, f32[8,64]{1,0:T(8,128)S(1)} %log_add_fusion.1, pred[64,8192]{1,0:T(8,128)(4,1)S(1)} %get-tuple-element.10, bf16[8192,256]{1,0:T(8,128)(2,1)S(1)} %copy-done.2), kind=kOutput, calls=%fused_computation.40 | convolution fusion | flops 6455099392 | bytes 19533824 | tf_op jit(solution)/shard_map/hqk,kd->qhd/dot_general | solution.py:99
  333.5 0.1 copy.16
  333.6 0.1 concatenate.25
  333.7 14.7 %fusion.36 = bf16[64,8,128]{2,0,1:T(8,128)(2,1)S(1)} fusion(f32[8192,64,8]{0,1,2:T(8,128)} %copy-done, f32[8,64]{1,0:T(8,128)S(1)} %log_add_fusion, pred[64,8192]{1,0:T(8,128)(4,1)S(1)} %get-tuple-element.11, bf16[8192,256]{1,0:T(8,128)(2,1)} %all-gather.5.cloned.1.call-done), kind=kOutput, calls=%fused_computation.39 | convolution fusion | flops 6455099392 | bytes 19531776 | tf_op jit(solution)/shard_map/hqk,kd->qhd/dot_general | solution.py:99
  348.4 0.1 copy.18
  348.5 0.1 concatenate.26
  348.6 0.7 pad_maximum_fusion
  349.3 0.7 maximum_bitcast_fusion
  (11 shorter events, 0.2 us)
Async XLA Ops:
  7.2 163.0 %all-gather.3.cloned.1.call-start = ((), (), s32[]{:S(2)}) async-start(), calls=%async_computation | async-start | bytes 4259840 | tf_op jit(solution)/shard_map/all_gather | solution.py:74
  7.9 284.5 %all-gather.5.cloned.1.call-start = ((), (), s32[]{:S(2)}) async-start(), calls=%async_computation.1 | async-start | bytes 4259840 | tf_op jit(solution)/shard_map/all_gather | solution.py:129
  7.9 32.9 %collective-permute-start = (bf16[1,128,2048]{2,1,0:T(8,128)(2,1)}, bf16[1,128,2048]{2,1,0:T(8,128)(2,1)S(1)}, u32[]{:S(2)}, u32[]{:S(2)}) collective-permute-start(bf16[1,128,2048]{2,1,0:T(8,128)(2,1)} %param.5), channel_id=1, source_target_pairs={{0,256},{256,0},{1,257},{257,1},{2,258},{258,2},{3,259},{259,3},{4... | collective-permute-start | bytes 1572872 | tf_op jit(solution)/shard_map/ppermute | solution.py:33
  40.8 11.1 %collective-permute-start.1 = (bf16[1,128,2048]{2,1,0:T(8,128)(2,1)S(1)}, bf16[1,128,2048]{2,1,0:T(8,128)(2,1)S(1)}, u32[]{:S(2)}, u32[]{:S(2)}) collective-permute-start(bf16[1,128,2048]{2,1,0:T(8,128)(2,1)S(1)} %collective-permute-done), channel_id=1, source_target_pairs={{0,1},{1,2},{2,3},{3,0},{4,5},{5,6},{6,7},{7,4},{8,9},{9,10},{10,1... | collective-permute-start | bytes 1572872 | tf_op jit(solution)/shard_map/ppermute | solution.py:21
  44.0 126.1 %copy-start.3 = (f32[1,8192]{1,0:T(1,128)S(1)}, f32[1,8192]{1,0:T(1,128)}, u32[]{:S(2)}) copy-start(f32[1,8192]{1,0:T(1,128)} %param.6) | copy-start | bytes 98308
  44.0 10.3 %collective-permute-start.2 = (bf16[1,128,2048]{2,1,0:T(8,128)(2,1)S(1)}, bf16[1,128,2048]{2,1,0:T(8,128)(2,1)S(1)}, u32[]{:S(2)}, u32[]{:S(2)}) collective-permute-start(bf16[1,128,2048]{2,1,0:T(8,128)(2,1)S(1)} %collective-permute-done), channel_id=1, source_target_pairs={{0,3},{1,0},{2,1},{3,2},{4,7},{5,4},{6,5},{7,6},{8,11},{9,8},{10,9... | collective-permute-start | bytes 1572872 | tf_op jit(solution)/shard_map/ppermute | solution.py:24
  52.0 11.1 %collective-permute-start.3 = (bf16[1,128,2048]{2,1,0:T(8,128)(2,1)S(1)}, bf16[1,128,2048]{2,1,0:T(8,128)(2,1)S(1)}, u32[]{:S(2)}, u32[]{:S(2)}) collective-permute-start(bf16[1,128,2048]{2,1,0:T(8,128)(2,1)S(1)} %collective-permute-done.1), channel_id=1, source_target_pairs={{0,1},{1,2},{2,3},{3,0},{4,5},{5,6},{6,7},{7,4},{8,9},{9,10},{10,1... | collective-permute-start | bytes 1572872 | tf_op jit(solution)/shard_map/ppermute | solution.py:21
  170.1 4.5 %copy-start.1 = (bf16[1,128,1024]{2,1,0:T(8,128)(2,1)S(1)}, bf16[1,128,1024]{2,1,0:T(8,128)(2,1)}, u32[]{:S(2)}) copy-start(bf16[1,128,1024]{2,1,0:T(8,128)(2,1)} %param.8) | copy-start | bytes 786436
  292.4 4.8 %copy-start.2 = (bf16[8192,256]{1,0:T(8,128)(2,1)S(1)}, bf16[8192,256]{1,0:T(8,128)(2,1)}, u32[]{:S(2)}) copy-start(bf16[8192,256]{1,0:T(8,128)(2,1)} %all-gather.5.cloned.1.call-done) | copy-start | bytes 12582916
  297.2 10.7 %copy-start = (f32[8192,64,8]{0,1,2:T(8,128)}, f32[8192,64,8]{0,1,2:T(8,128)S(1)}, u32[]{:S(2)}) copy-start(f32[8192,64,8]{0,1,2:T(8,128)S(1)} %get-tuple-element.15) | copy-start | bytes 50331652
Sparse Core Ops, SparseCore 0:
  10.1 159.9 all-gather.2
  174.8 117.5 all-gather.4
